TPU v7x, 32 devices: a whole 2x2x4 slice. The times are simulated.
32 devices in a mesh: fsdp: 8 (over z, y), rep: 4 (over x, core).
Axes of the slice: x: 2, y: 2, z: 4, core: 2. Of those that a mesh axis runs over, the one named last changes fastest.
Arguments:
- tokens: bfloat16 [32768, 768], P(('fsdp', 'rep')), may hold values from -6 to 6
- seg_ids: int32 [64, 512], P(('fsdp', 'rep')), may hold values from 0 to 3, never falling along the last dimension, each value on 1 to 256 neighbouring positions
- w_qkv: bfloat16 [768, 2304], P(('fsdp', 'rep')), may hold values from -0.21875 to 0.21875
- w_out: bfloat16 [768, 768], P(('fsdp', 'rep')), may hold values from -1.25 to 1.25
- w_up: bfloat16 [768, 3072], P(('fsdp', 'rep')), may hold values from -0.21875 to 0.21875
- w_down: bfloat16 [3072, 768], P(('fsdp', 'rep')), may hold values from -0.109375 to 0.109375
- ln_gain: bfloat16 [2, 768], P(None, ('fsdp', 'rep')), may hold values from 0.099609375 to 1.8984375
- ln_bias: bfloat16 [2, 768], P(None, ('fsdp', 'rep')), may hold values from -3 to 3
- bias_attn: bfloat16 [3, 768], P(None, ('fsdp', 'rep')), may hold values from -3 to 3
- bias_up: bfloat16 [3072], P(('fsdp', 'rep')), may hold values from -3 to 3
- bias_down: bfloat16 [768], P(('fsdp', 'rep')), may hold values from -3 to 3
- grad_out: bfloat16 [32768, 768], P(('fsdp', 'rep')), may hold values from -6 to 6
Outputs:
- layer_out: bfloat16 [32768, 768], P(('fsdp', 'rep'))
- grad_tokens: bfloat16 [32768, 768], P(('fsdp', 'rep'))
- grad_w_qkv: float32 [768, 2304], P(('fsdp', 'rep'))
- grad_w_out: float32 [768, 768], P(('fsdp', 'rep'))
- grad_w_up: float32 [768, 3072], P(('fsdp', 'rep'))
- grad_w_down: float32 [3072, 768], P(('fsdp', 'rep'))
- grad_ln_gain: float32 [2, 768], P(None, ('fsdp', 'rep'))
- grad_ln_bias: float32 [2, 768], P(None, ('fsdp', 'rep'))
- grad_bias_attn: float32 [3, 768], P(None, ('fsdp', 'rep'))
- grad_bias_up: float32 [3072], P(('fsdp', 'rep'))
- grad_bias_down: float32 [768], P(('fsdp', 'rep'))
Inputs may be any that keep to these rules, and one draw needn't show every extreme that they name: `seg_ids`: within each row (one micro-batch of 512 tokens) sequence numbers never fall; each sequence has 1 to 256 tokens and one has exactly 256.
All inputs are finite; a program needn't handle non-finite values.
Results may differ from a plain program's by a relative error of at most 0.012.
Values may be sent and summed in bfloat16 or wider, within the bound.
A program may use at most 192 MiB of HBM per device.

v0:
```python
import jax
import jax.numpy as jnp
from jax import lax
from jax.sharding import PartitionSpec as P

HEAD = 64


EPSILON = 1e-05
SCORE_SCALE = 0.125
MASK_VALUE = -1000000000.0


def norm_rows(inputs, scaling, offset):
    row_mean = jnp.mean(inputs, axis=-1, keepdims=True)
    centred = inputs - row_mean
    spread = jnp.mean(centred * centred, axis=-1, keepdims=True)
    return centred * lax.rsqrt(spread + EPSILON) * scaling + offset


def fetch(w_qkv, w_out, w_up, w_down, ln_gain, ln_bias, bias_attn, bias_up, bias_down):
    return (
        lax.all_gather(w_qkv, ("fsdp", "rep"), axis=0, tiled=True),
        lax.all_gather(w_out, ("fsdp", "rep"), axis=0, tiled=True),
        lax.all_gather(w_up, ("fsdp", "rep"), axis=0, tiled=True),
        lax.all_gather(w_down, ("fsdp", "rep"), axis=0, tiled=True),
        lax.all_gather(ln_gain, ("fsdp", "rep"), axis=1, tiled=True),
        lax.all_gather(ln_bias, ("fsdp", "rep"), axis=1, tiled=True),
        lax.all_gather(bias_attn, ("fsdp", "rep"), axis=1, tiled=True),
        lax.all_gather(bias_up, ("fsdp", "rep"), axis=0, tiled=True),
        lax.all_gather(bias_down, ("fsdp", "rep"), axis=0, tiled=True),
    )


def settle(qkv_sum, out_sum, up_sum, down_sum, gain_sum, shift_sum, attn_sum, upb_sum, downb_sum):
    return (
        lax.psum_scatter(qkv_sum, ("fsdp", "rep"), scatter_dimension=0, tiled=True),
        lax.psum_scatter(out_sum, ("fsdp", "rep"), scatter_dimension=0, tiled=True),
        lax.psum_scatter(up_sum, ("fsdp", "rep"), scatter_dimension=0, tiled=True),
        lax.psum_scatter(down_sum, ("fsdp", "rep"), scatter_dimension=0, tiled=True),
        lax.psum_scatter(gain_sum, ("fsdp", "rep"), scatter_dimension=1, tiled=True),
        lax.psum_scatter(shift_sum, ("fsdp", "rep"), scatter_dimension=1, tiled=True),
        lax.psum_scatter(attn_sum, ("fsdp", "rep"), scatter_dimension=1, tiled=True),
        lax.psum_scatter(upb_sum, ("fsdp", "rep"), scatter_dimension=0, tiled=True),
        lax.psum_scatter(downb_sum, ("fsdp", "rep"), scatter_dimension=0, tiled=True),
    )


def allowed_pairs(segment_row):
    row_count = segment_row.shape[0]
    places = lax.broadcasted_iota(jnp.int32, (row_count, row_count), 0)
    others = lax.broadcasted_iota(jnp.int32, (row_count, row_count), 1)
    return (segment_row[:, None] == segment_row[None, :]) & (others <= places)


def scores_of(queries, key_rows, allowed):
    raw_scores = (
        jnp.einsum("qhd,khd->hqk", queries, key_rows, preferred_element_type=jnp.float32)
        * SCORE_SCALE
    )
    return jnp.where(allowed[None], raw_scores, MASK_VALUE)


def forward_block(params, token_rows, segment_row):
    w_qkv, w_out, w_up, w_down, ln_gain, ln_bias, bias_attn, bias_up, bias_down = params
    row_count = token_rows.shape[0]
    model_width = token_rows.shape[1]
    head_count = model_width // HEAD
    gains = ln_gain.astype(jnp.float32)
    shifts = ln_bias.astype(jnp.float32)
    attn_bias = bias_attn.astype(jnp.float32)
    rows_float = token_rows.astype(jnp.float32)
    normed, norm_one = jax.vjp(norm_rows, rows_float, gains[0], shifts[0])
    normed_low = normed.astype(jnp.bfloat16)
    zero_bias = jnp.zeros((model_width,), jnp.float32)
    qkv_bias = jnp.concatenate([attn_bias[0], zero_bias, attn_bias[1]])
    joined = (jnp.dot(normed_low, w_qkv, preferred_element_type=jnp.float32) + qkv_bias).astype(
        jnp.bfloat16
    )
    queries = joined[:, :model_width].reshape(row_count, head_count, HEAD)
    key_rows = joined[:, model_width : 2 * model_width].reshape(row_count, head_count, HEAD)
    values = joined[:, 2 * model_width :].reshape(row_count, head_count, HEAD)
    allowed = allowed_pairs(segment_row)
    scores = scores_of(queries, key_rows, allowed)
    row_max = jnp.max(scores, axis=-1, keepdims=True)
    exp_scores = jnp.exp(scores - row_max)
    row_sum = jnp.sum(exp_scores, axis=-1, keepdims=True)
    attn_probs = (exp_scores / row_sum).astype(jnp.bfloat16)
    log_norm = row_max + jnp.log(row_sum)
    attended = jnp.einsum("hqk,khd->qhd", attn_probs, values, preferred_element_type=jnp.float32)
    attended = attended.reshape(row_count, model_width).astype(jnp.bfloat16)
    residual = (
        rows_float + jnp.dot(attended, w_out, preferred_element_type=jnp.float32) + attn_bias[2]
    )
    second, norm_two = jax.vjp(norm_rows, residual, gains[1], shifts[1])
    second_low = second.astype(jnp.bfloat16)
    pre_act = jnp.dot(second_low, w_up, preferred_element_type=jnp.float32) + bias_up.astype(
        jnp.float32
    )
    active, gelu_back = jax.vjp(jax.nn.gelu, pre_act)
    active_low = active.astype(jnp.bfloat16)
    layer_rows = (
        residual
        + jnp.dot(active_low, w_down, preferred_element_type=jnp.float32)
        + bias_down.astype(jnp.float32)
    )
    saved_state = (
        norm_one,
        normed_low,
        queries,
        key_rows,
        values,
        allowed,
        log_norm,
        attended,
        norm_two,
        second_low,
        gelu_back,
        active_low,
    )
    return (layer_rows.astype(jnp.bfloat16), saved_state)


def backward_block(params, saved_state, grad_rows, totals):
    w_qkv, w_out, w_up, w_down, ln_gain, ln_bias, bias_attn, bias_up, bias_down = params
    (
        norm_one,
        normed_low,
        queries,
        key_rows,
        values,
        allowed,
        log_norm,
        attended,
        norm_two,
        second_low,
        gelu_back,
        active_low,
    ) = saved_state
    qkv_sum, out_sum, up_sum, down_sum, gain_sum, shift_sum, attn_sum, upb_sum, downb_sum = totals
    row_count = grad_rows.shape[0]
    model_width = grad_rows.shape[1]
    head_count = model_width // HEAD
    grad_float = grad_rows.astype(jnp.float32)
    down_sum = down_sum + jnp.einsum(
        "nf,nd->fd", active_low, grad_rows, preferred_element_type=jnp.float32
    )
    downb_sum = downb_sum + jnp.sum(grad_float, axis=0)
    grad_active = jnp.einsum("nd,fd->nf", grad_rows, w_down, preferred_element_type=jnp.float32)
    grad_pre = gelu_back(grad_active)[0].astype(jnp.bfloat16)
    up_sum = up_sum + jnp.einsum(
        "nd,nf->df", second_low, grad_pre, preferred_element_type=jnp.float32
    )
    upb_sum = upb_sum + jnp.sum(grad_pre.astype(jnp.float32), axis=0)
    grad_second = jnp.einsum("nf,df->nd", grad_pre, w_up, preferred_element_type=jnp.float32)
    grad_resid, gain_two, shift_two = norm_two(grad_second)
    grad_resid = grad_resid + grad_float
    grad_resid_low = grad_resid.astype(jnp.bfloat16)
    out_sum = out_sum + jnp.einsum(
        "nc,nd->cd", attended, grad_resid_low, preferred_element_type=jnp.float32
    )
    bias_out_grad = jnp.sum(grad_resid_low.astype(jnp.float32), axis=0)
    grad_att = jnp.einsum("nd,cd->nc", grad_resid_low, w_out, preferred_element_type=jnp.float32)
    grad_att = grad_att.astype(jnp.bfloat16).reshape(row_count, head_count, HEAD)
    scores = scores_of(queries, key_rows, allowed)
    attn_probs = jnp.exp(scores - log_norm)
    probs_low = attn_probs.astype(jnp.bfloat16)
    grad_probs = jnp.einsum("qhd,khd->hqk", grad_att, values, preferred_element_type=jnp.float32)
    grad_scores = attn_probs * (
        grad_probs - jnp.sum(attn_probs * grad_probs, axis=-1, keepdims=True)
    )
    grad_scores = grad_scores.astype(jnp.bfloat16)
    grad_query = (
        jnp.einsum("hqk,khd->qhd", grad_scores, key_rows, preferred_element_type=jnp.float32)
        * SCORE_SCALE
    )
    grad_keys = (
        jnp.einsum("hqk,qhd->khd", grad_scores, queries, preferred_element_type=jnp.float32)
        * SCORE_SCALE
    )
    grad_values = jnp.einsum(
        "hqk,qhd->khd", probs_low, grad_att, preferred_element_type=jnp.float32
    )
    grad_joined = jnp.concatenate(
        [
            grad_query.reshape(row_count, model_width),
            grad_keys.reshape(row_count, model_width),
            grad_values.reshape(row_count, model_width),
        ],
        axis=1,
    ).astype(jnp.bfloat16)
    qkv_sum = qkv_sum + jnp.einsum(
        "nd,ne->de", normed_low, grad_joined, preferred_element_type=jnp.float32
    )
    joined_float = grad_joined.astype(jnp.float32)
    attn_terms = jnp.stack(
        [
            jnp.sum(joined_float[:, :model_width], axis=0),
            jnp.sum(joined_float[:, 2 * model_width :], axis=0),
            bias_out_grad,
        ]
    )
    attn_sum = attn_sum + attn_terms
    grad_normed = jnp.einsum("ne,de->nd", grad_joined, w_qkv, preferred_element_type=jnp.float32)
    grad_input, gain_one, shift_one = norm_one(grad_normed)
    gain_sum = gain_sum + jnp.stack([gain_one, gain_two])
    shift_sum = shift_sum + jnp.stack([shift_one, shift_two])
    grad_input = (grad_resid + grad_input).astype(jnp.bfloat16)
    return (
        grad_input,
        (qkv_sum, out_sum, up_sum, down_sum, gain_sum, shift_sum, attn_sum, upb_sum, downb_sum),
    )


def local(
    tokens,
    seg_ids,
    w_qkv,
    w_out,
    w_up,
    w_down,
    ln_gain,
    ln_bias,
    bias_attn,
    bias_up,
    bias_down,
    grad_out,
):
    batches = seg_ids.shape[0]
    length = seg_ids.shape[1]
    model_width = tokens.shape[1]
    token_blocks = tokens.reshape(batches, length, model_width)
    grad_blocks = grad_out.reshape(batches, length, model_width)
    outputs = []
    saved_all = []
    for index in range(batches):
        params = fetch(w_qkv, w_out, w_up, w_down, ln_gain, ln_bias, bias_attn, bias_up, bias_down)
        layer_rows, saved_state = forward_block(params, token_blocks[index], seg_ids[index])
        outputs.append(layer_rows)
        saved_all.append(saved_state)
    totals = tuple((jnp.zeros(tensor.shape, jnp.float32) for tensor in params))
    grad_list = []
    for index in range(batches):
        params = fetch(w_qkv, w_out, w_up, w_down, ln_gain, ln_bias, bias_attn, bias_up, bias_down)
        grad_input, totals = backward_block(params, saved_all[index], grad_blocks[index], totals)
        grad_list.append(grad_input)
    settled = settle(
        totals[0],
        totals[1],
        totals[2],
        totals[3],
        totals[4],
        totals[5],
        totals[6],
        totals[7],
        totals[8],
    )
    layer_out = jnp.concatenate(outputs, axis=0)
    grad_tokens = jnp.concatenate(grad_list, axis=0)
    return (
        layer_out,
        grad_tokens,
        settled[0],
        settled[1],
        settled[2],
        settled[3],
        settled[4],
        settled[5],
        settled[6],
        settled[7],
        settled[8],
    )


def solution(mesh):
    return jax.shard_map(
        local,
        mesh=mesh,
        in_specs=(
            P(("fsdp", "rep"), None),
            P(("fsdp", "rep"), None),
            P(("fsdp", "rep"), None),
            P(("fsdp", "rep"), None),
            P(("fsdp", "rep"), None),
            P(("fsdp", "rep"), None),
            P(None, ("fsdp", "rep")),
            P(None, ("fsdp", "rep")),
            P(None, ("fsdp", "rep")),
            P(("fsdp", "rep")),
            P(("fsdp", "rep")),
            P(("fsdp", "rep"), None),
        ),
        out_specs=(
            P(("fsdp", "rep"), None),
            P(("fsdp", "rep"), None),
            P(("fsdp", "rep"), None),
            P(("fsdp", "rep"), None),
            P(("fsdp", "rep"), None),
            P(("fsdp", "rep"), None),
            P(None, ("fsdp", "rep")),
            P(None, ("fsdp", "rep")),
            P(None, ("fsdp", "rep")),
            P(("fsdp", "rep")),
            P(("fsdp", "rep")),
        ),
        check_vma=False,
    )
```

profile of v0, /device:TPU:0, one launch (start us, length us, event | category | flops | bytes accessed | tf_op | source)
XLA Modules:
  0.0 842.9 jit_solution(154464425881189074)
XLA Ops:
  15.1 42.3 %all-reduce.8 = (bf16[768]{0:T(1024)(128)(2,1)}, bf16[3072]{0:T(1024)(128)(2,1)S(1)}) all-reduce(bf16[768]{0:T(1024)(128)(2,1)S(1)} %dynamic-update-slice.1, bf16[3072]{0:T(1024)(128)(2,1)S(1)} %dynamic-update-slice), channel_id=1, replica_groups=mesh['fsdp'=8,'rep'=4] {'fsdp','rep'}, use_global_device_ids=true, to_apply=%add.1 | all-reduce | flops 3840 | bytes 15360
  58.0 40.2 %all-gather = bf16[32,24,2]{1,2,0:T(2,128)(2,1)S(1)} all-gather(bf16[1,24,2]{1,2,0:T(2,128)(2,1)S(1)} %bitcast.156), channel_id=1, replica_groups=mesh['fsdp'=8,'rep'=4] {'fsdp','rep'}, dimensions={0}, use_global_device_ids=true | all-gather | bytes 3168 | tf_op jit(solution)/shard_map/all_gather | solution.py:27
  98.3 36.4 %all-gather.1 = bf16[32,24,2]{1,2,0:T(2,128)(2,1)S(1)} all-gather(bf16[1,24,2]{1,2,0:T(2,128)(2,1)S(1)} %bitcast.157), channel_id=1, replica_groups=mesh['fsdp'=8,'rep'=4] {'fsdp','rep'}, dimensions={0}, use_global_device_ids=true | all-gather | bytes 3168 | tf_op jit(solution)/shard_map/all_gather | solution.py:28
  135.2 38.2 %all-gather.2 = bf16[32,24,3]{1,2,0:T(4,128)(2,1)S(1)} all-gather(bf16[1,24,3]{1,2,0:T(4,128)(2,1)S(1)} %bitcast.155), channel_id=1, replica_groups=mesh['fsdp'=8,'rep'=4] {'fsdp','rep'}, dimensions={0}, use_global_device_ids=true | all-gather | bytes 4752 | tf_op jit(solution)/shard_map/all_gather | solution.py:29
  175.1 4.5 fusion.27
  182.3 2.6 copy.96
  186.1 4.3 fusion.26
  193.2 2.7 copy.92
  195.9 2.3 copy.91
  198.2 3.3 fusion.28
  201.5 3.8 fusion
  206.0 5.7 fusion.61
  211.7 2.5 fusion.111
  217.5 2.6 fusion.1
  222.0 4.0 fusion.60
  228.0 8.3 fusion.101
  236.2 4.8 fusion.102
  241.1 19.1 %all-gather.14.cloned.1.call-done = bf16[3072,768]{1,0:T(8,128)(2,1)} async-done(((bf16[96,768]{1,0:T(8,128)(2,1)}), bf16[3072,768]{1,0:T(8,128)(2,1)}) %all-gather.14.cloned.1.call-update) | async-done | bytes 4718608 | tf_op jit(solution)/shard_map/all_gather | solution.py:26
  260.2 9.8 %convert_reduce_fusion.1 = (f32[3072]{0:T(1024)}, bf16[512,3072]{1,0:T(8,128)(2,1)S(1)}) fusion(f32[512,3072]{1,0:T(8,128)} %fusion.101, f32[3072]{0:T(1024)S(1)} %copy-done.84, bf16[3072,768]{1,0:T(8,128)(2,1)} %all-gather.14.cloned.1.call-done, bf16[1024,768]{1,0:T(8,128)(2,1)} %param.23), kind=kOutput, calls=%fused_computation.37 | convolution fusion | flops 2452091904 | bytes 14966784 | tf_op jit(solution)/shard_map/nd,fd->nf/dot_general | solution.py:149
  270.1 7.2 convert_reduce_fusion
  277.3 2.7 fusion.112
  280.1 3.8 multiply_reduce_fusion.3
  290.2 2.3 copy.103
  292.5 13.7 %multiply_reduce_fusion = (f32[12,512]{1,0:T(8,128)S(1)}, f32[12,512,512]{1,2,0:T(8,128)}) fusion(f32[12,512]{1,0:T(8,128)S(1)} %log_add_fusion, f32[12,512,512]{1,2,0:T(8,128)} %copy-done.1, pred[512,512]{0,1:T(8,128)(4,1)S(1)} %fusion.62, bf16[512,12,64]{0,2,1:T(8,128)(2,1)} %bitcast.133, bf16[512,12,64]{0,2,1:T(8,128)(2,1)} %bitcast.131), kind=kOutput, calls=%fused_computation.1 | convolution fusion | flops 418375680 | bytes 27049984 | tf_op jit(solution)/shard_map/qhd,khd->hqk/dot_general | solution.py:168
  306.2 7.3 multiply_convert_fusion
  313.5 2.9 multiply_convert_fusion.4
  318.5 2.2 fusion.113
  322.3 2.3 copy.99
  324.7 4.4 convolution_add_fusion.5
  329.1 13.8 %multiply_reduce_fusion.1 = (f32[12,512]{1,0:T(8,128)S(1)}, f32[12,512,512]{1,2,0:T(8,128)}) fusion(f32[12,512]{1,0:T(8,128)S(1)} %log_add_fusion.1, f32[12,512,512]{1,2,0:T(8,128)} %copy-done, pred[512,512]{0,1:T(8,128)(4,1)S(1)} %copy-done.21, bf16[512,12,64]{0,2,1:T(8,128)(2,1)} %bitcast.135, bf16[512,12,64]{0,2,1:T(8,128)(2,1)} %bitcast.130), kind=kOutput, calls=%fused_computation.4 | convolution fusion | flops 418375680 | bytes 27049984 | tf_op jit(solution)/shard_map/qhd,khd->hqk/dot_general | solution.py:168
  342.9 7.5 multiply_convert_fusion.1
  350.5 2.9 multiply_convert_fusion.6
  355.4 4.0 fusion.54
  359.4 4.2 fusion.89
  363.7 3.9 fusion.57
  367.6 6.4 convolution_add_fusion
  374.7 7.1 fusion.71
  381.9 10.2 %convolution_add_fusion.1 = f32[3072,768]{1,0:T(8,128)} fusion(f32[3072,768]{1,0:T(8,128)S(1)} %fusion.71, bf16[1024,768]{1,0:T(8,128)(2,1)S(1)} %copy-done.25, f32[512,3072]{1,0:T(8,128)} %fusion.102, f32[3072]{0:T(1024)S(1)} %copy-done.85), kind=kOutput, calls=%fused_computation.45 | convolution fusion | flops 2434007040 | bytes 25964544 | tf_op jit(solution)/shard_map/nf,nd->fd/dot_general | solution.py:145
  392.8 5.4 fusion.100
  398.2 6.0 convolution_add_fusion.2
  405.0 2.4 fusion.94
  411.3 2.7 fusion.49
  417.2 40.6 %all-reduce.7 = (f32[2,768]{1,0:T(2,128)S(1)}, f32[2,768]{1,0:T(2,128)S(1)}, f32[3,768]{1,0:T(4,128)S(1)}, f32[3072]{0:T(1024)S(1)}, f32[768]{0:T(1024)S(1)}) all-reduce(f32[2,768]{1,0:T(2,128)S(1)} %maximum_add_fusion.1, f32[2,768]{1,0:T(2,128)S(1)} %maximum_add_fusion.2, ...), channel_id=6, replica_groups=mesh['fsdp'=8,'rep'=4] {'fsdp','rep'}, use_global_device_ids=true, to_apply=%region_30.31.clone | all-reduce | flops 9216 | bytes 73728
  460.9 9.0 %add_convert_fusion.4 = bf16[512,768]{1,0:T(8,128)(2,1)S(1)} fusion(f32[512,768]{1,0:T(8,128)} %copy-done.31, bf16[3072,768]{1,0:T(8,128)(2,1)} %all-gather.14.cloned.1.call-done, f32[768]{0:T(1024)S(1)} %convert_element_type.155, f32[512,3072]{1,0:T(8,128)} %fusion.101, f32[3072]{0:T(1024)S(1)} %copy-done.85), kind=kOutput, calls=%fused_computation.115 | convolution fusion | flops 2432827392 | bytes 13384704 | tf_op jit(solution)/shard_map/dot_general | solution.py:104
  470.0 8.6 %add_convert_fusion.2 = bf16[512,768]{1,0:T(8,128)(2,1)S(1)} fusion(f32[512,768]{1,0:T(8,128)S(1)} %get-tuple-element.81, bf16[3072,768]{1,0:T(8,128)(2,1)} %all-gather.14.cloned.1.call-done, f32[768]{0:T(1024)S(1)} %convert_element_type.155, f32[512,3072]{1,0:T(8,128)} %fusion.102, f32[3072]{0:T(1024)S(1)} %copy-done.85), kind=kOutput, calls=%fused_computation.112 | convolution fusion | flops 2432827392 | bytes 13384704 | tf_op jit(solution)/shard_map/dot_general | solution.py:104
  483.9 68.5 %reduce-scatter.8.cloned.1.call-done = f32[24,2304]{1,0:T(8,128)} async-done(((f32[768,2304]{1,0:T(8,128)}), f32[24,2304]{1,0:T(8,128)}) %reduce-scatter.8.cloned.1.call-update) | async-done | bytes 221200 | tf_op jit(solution)/shard_map/reduce_scatter | solution.py:37
  552.3 141.3 %reduce-scatter.14.cloned.1.call-done = f32[96,768]{1,0:T(8,128)} async-done(((f32[3072,768]{1,0:T(8,128)}), f32[96,768]{1,0:T(8,128)}) %reduce-scatter.14.cloned.1.call-update) | async-done | bytes 294928 | tf_op jit(solution)/shard_map/reduce_scatter | solution.py:40
  693.7 142.1 %reduce-scatter.12.cloned.1.call-done = f32[24,3072]{1,0:T(8,128)} async-done(((f32[768,3072]{1,0:T(8,128)}), f32[24,3072]{1,0:T(8,128)}) %reduce-scatter.12.cloned.1.call-update) | async-done | bytes 294928 | tf_op jit(solution)/shard_map/reduce_scatter | solution.py:39
  (350 shorter events, 54.2 us)
Async XLA Ops:
  7.2 167.9 %copy-start.2 = (bf16[1024,768]{1,0:T(8,128)(2,1)S(1)}, bf16[1024,768]{1,0:T(8,128)(2,1)}, u32[]{:S(2)}) copy-start(bf16[1024,768]{1,0:T(8,128)(2,1)} %param.12) | copy-start | bytes 4718596
  7.2 7.6 copy-start.105
  7.2 50.8 %copy-start.96 = (bf16[2,24]{1,0:T(2,128)(2,1)S(1)}, bf16[2,24]{1,0:T(2,128)(2,1)}, u32[]{:S(2)}) copy-start(bf16[2,24]{1,0:T(2,128)(2,1)} %param.18) | copy-start | bytes 292
  7.2 91.1 %copy-start.97 = (bf16[2,24]{1,0:T(2,128)(2,1)S(1)}, bf16[2,24]{1,0:T(2,128)(2,1)}, u32[]{:S(2)}) copy-start(bf16[2,24]{1,0:T(2,128)(2,1)} %param.19) | copy-start | bytes 292
  7.2 128.0 %copy-start.95 = (bf16[3,24]{1,0:T(4,128)(2,1)S(1)}, bf16[3,24]{1,0:T(4,128)(2,1)}, u32[]{:S(2)}) copy-start(bf16[3,24]{1,0:T(4,128)(2,1)} %param.20) | copy-start | bytes 436
  7.2 167.8 %all-gather.8.cloned.1.call-start = ((), (), s32[]{:S(2)}) async-start(), calls=%async_computation.4 | async-start | bytes 3649536 | tf_op jit(solution)/shard_map/all_gather | solution.py:23
  8.0 203.7 %all-gather.10.cloned.1.call-start = ((), (), s32[]{:S(2)}) async-start(), calls=%async_computation.5 | async-start | bytes 1216512 | tf_op jit(solution)/shard_map/all_gather | solution.py:24
  8.7 219.2 %all-gather.12.cloned.1.call-start = ((), (), s32[]{:S(2)}) async-start(), calls=%async_computation.6 | async-start | bytes 4866048 | tf_op jit(solution)/shard_map/all_gather | solution.py:25
  9.5 250.8 %all-gather.14.cloned.1.call-start = ((), (), s32[]{:S(2)}) async-start(), calls=%async_computation.7 | async-start | bytes 4866048 | tf_op jit(solution)/shard_map/all_gather | solution.py:26
  10.0 473.8 %reduce-scatter.10.cloned.1.call-start = ((), (), s32[]{:S(2)}) async-start(), calls=%async_computation.9 | async-start | bytes 2433024 | tf_op jit(solution)/shard_map/reduce_scatter | solution.py:38
  12.5 167.0 %copy-start.53 = (f32[512]{0:T(512)}, f32[512]{0:T(512)S(1)}, u32[]{:S(2)}) copy-start(f32[512]{0:T(512)S(1)} %get-tuple-element.96) | copy-start | bytes 6148
  12.5 173.5 %copy-start.59 = (f32[512]{0:T(512)}, f32[512]{0:T(512)S(1)}, u32[]{:S(2)}) copy-start(f32[512]{0:T(512)S(1)} %get-tuple-element.97) | copy-start | bytes 6148
  14.5 120.3 %copy-start.72 = (f32[512]{0:T(512)}, f32[512]{0:T(512)S(1)}, u32[]{:S(2)}) copy-start(f32[512]{0:T(512)S(1)} %get-tuple-element.34) | copy-start | bytes 6148
  14.5 120.3 %copy-start.74 = (f32[512]{0:T(512)}, f32[512]{0:T(512)S(1)}, u32[]{:S(2)}) copy-start(f32[512]{0:T(512)S(1)} %get-tuple-element.33) | copy-start | bytes 6148
  14.5 171.5 %copy-start.63 = (f32[512]{0:T(512)}, f32[512]{0:T(512)S(1)}, u32[]{:S(2)}) copy-start(f32[512]{0:T(512)S(1)} %fusion.77) | copy-start | bytes 6148
  14.6 165.0 %copy-start.57 = (f32[512]{0:T(512)}, f32[512]{0:T(512)S(1)}, u32[]{:S(2)}) copy-start(f32[512]{0:T(512)S(1)} %fusion.79) | copy-start | bytes 6148
  174.0 132.2 %copy-start.18 = (pred[512,512]{0,1:T(8,128)(4,1)}, pred[512,512]{0,1:T(8,128)(4,1)S(1)}, u32[]{:S(2)}) copy-start(pred[512,512]{0,1:T(8,128)(4,1)S(1)} %fusion.62) | copy-start | bytes 786436
  174.9 11.1 %copy-start.45 = (f32[768]{0:T(1024)}, f32[768]{0:T(1024)S(1)}, u32[]{:S(2)}) copy-start(f32[768]{0:T(1024)S(1)} %get-tuple-element.98) | copy-start | bytes 9220
  175.0 11.1 %copy-start.51 = (f32[768]{0:T(1024)}, f32[768]{0:T(1024)S(1)}, u32[]{:S(2)}) copy-start(f32[768]{0:T(1024)S(1)} %get-tuple-element.43) | copy-start | bytes 9220
  175.0 61.3 %copy-start.49 = (f32[768]{0:T(1024)}, f32[768]{0:T(1024)S(1)}, u32[]{:S(2)}) copy-start(f32[768]{0:T(1024)S(1)} %get-tuple-element.42) | copy-start | bytes 9220
  175.0 108.9 %copy-start.47 = (f32[768]{0:T(1024)}, f32[768]{0:T(1024)S(1)}, u32[]{:S(2)}) copy-start(f32[768]{0:T(1024)S(1)} %get-tuple-element.99) | copy-start | bytes 9220
  182.2 33.1 %copy-start.9 = (bf16[512,768]{0,1:T(8,128)(2,1)}, bf16[512,768]{0,1:T(8,128)(2,1)S(1)}, u32[]{:S(2)}) copy-start(bf16[512,768]{0,1:T(8,128)(2,1)S(1)} %copy.97) | copy-start | bytes 2359300
  193.2 8.3 copy-start.7
  214.5 12.8 %copy-start.76 = (f32[512]{0:T(512)}, f32[512]{0:T(512)S(1)}, u32[]{:S(2)}) copy-start(f32[512]{0:T(512)S(1)} %multiply_reduce_fusion.7) | copy-start | bytes 6148
  227.0 56.9 %copy-start.55 = (f32[512]{0:T(512)}, f32[512]{0:T(512)S(1)}, u32[]{:S(2)}) copy-start(f32[512]{0:T(512)S(1)} %broadcast_multiply_fusion) | copy-start | bytes 6148
  227.9 56.1 %copy-start.61 = (f32[512]{0:T(512)}, f32[512]{0:T(512)S(1)}, u32[]{:S(2)}) copy-start(f32[512]{0:T(512)S(1)} %fusion.80) | copy-start | bytes 6148
  228.0 8.3 copy-start.99
  236.2 24.0 %copy-start.84 = (f32[3072]{0:T(1024)S(1)}, f32[3072]{0:T(1024)}, u32[]{:S(2)}) copy-start(f32[3072]{0:T(1024)} %convert_element_type.153) | copy-start | bytes 36868
  260.2 9.8 %copy-start.24 = (bf16[1024,768]{1,0:T(8,128)(2,1)S(1)}, bf16[1024,768]{1,0:T(8,128)(2,1)}, u32[]{:S(2)}) copy-start(bf16[1024,768]{1,0:T(8,128)(2,1)} %param.23) | copy-start | bytes 4718596
  260.2 9.8 %copy-start.98 = (bf16[3072,768]{1,0:T(8,128)(2,1)S(1)}, bf16[3072,768]{1,0:T(8,128)(2,1)}, u32[]{:S(2)}) copy-start(bf16[3072,768]{1,0:T(8,128)(2,1)} %all-gather.14.cloned.1.call-done) | copy-start | bytes 14155780
  260.2 9.8 %copy-start.106 = (f32[512,3072]{1,0:T(8,128)S(1)}, f32[512,3072]{1,0:T(8,128)}, u32[]{:S(2)}) copy-start(f32[512,3072]{1,0:T(8,128)} %fusion.102) | copy-start | bytes 18874372
  260.2 17.0 %slice-start.9 = ((s8[4718592]{0:T(1024)(128)(4,1)}), s8[4194304]{0:T(1024)(128)(4,1)S(1)}, s32[]{:S(2)}) async-start(s8[4718592]{0:T(1024)(128)(4,1)} %bitcast.158), calls=%async_computation.21 | async-start | bytes 8388608
  270.1 9.9 %copy-start.107 = (bf16[512,3072]{1,0:T(8,128)(2,1)}, bf16[512,3072]{1,0:T(8,128)(2,1)S(1)}, u32[]{:S(2)}) copy-start(bf16[512,3072]{1,0:T(8,128)(2,1)S(1)} %get-tuple-element.93) | copy-start | bytes 9437188
  292.5 13.7 %slice-start.3 = ((s8[12582912]{0:T(1024)(128)(4,1)}), s8[4194304]{0:T(1024)(128)(4,1)S(1)}, s32[]{:S(2)}) async-start(s8[12582912]{0:T(1024)(128)(4,1)} %bitcast.108), calls=%async_computation.15 | async-start | bytes 8388608
  292.5 13.7 %slice-start.4 = ((s8[12582912]{0:T(1024)(128)(4,1)}), s8[4194304]{0:T(1024)(128)(4,1)S(1)}, s32[]{:S(2)}) async-start(s8[12582912]{0:T(1024)(128)(4,1)} %bitcast.108), calls=%async_computation.16 | async-start | bytes 8388608
  292.5 13.7 %slice-start.5 = ((s8[12582912]{0:T(1024)(128)(4,1)}), s8[4194304]{0:T(1024)(128)(4,1)S(1)}, s32[]{:S(2)}) async-start(s8[12582912]{0:T(1024)(128)(4,1)} %bitcast.108), calls=%async_computation.17 | async-start | bytes 8388608
  329.0 223.3 %reduce-scatter.8.cloned.1.call-start = ((), (), s32[]{:S(2)}) async-start(), calls=%async_computation.8 | async-start | bytes 7299072 | tf_op jit(solution)/shard_map/reduce_scatter | solution.py:37
  329.1 13.8 %slice-start = ((s8[12582912]{0:T(1024)(128)(4,1)}), s8[4194304]{0:T(1024)(128)(4,1)S(1)}, s32[]{:S(2)}) async-start(s8[12582912]{0:T(1024)(128)(4,1)} %bitcast.106), calls=%async_computation.12 | async-start | bytes 8388608
  329.1 13.8 %slice-start.1 = ((s8[12582912]{0:T(1024)(128)(4,1)}), s8[4194304]{0:T(1024)(128)(4,1)S(1)}, s32[]{:S(2)}) async-start(s8[12582912]{0:T(1024)(128)(4,1)} %bitcast.106), calls=%async_computation.13 | async-start | bytes 8388608
  329.1 13.8 %slice-start.2 = ((s8[12582912]{0:T(1024)(128)(4,1)}), s8[4194304]{0:T(1024)(128)(4,1)S(1)}, s32[]{:S(2)}) async-start(s8[12582912]{0:T(1024)(128)(4,1)} %bitcast.106), calls=%async_computation.14 | async-start | bytes 8388608
  342.9 7.5 copy-start.13
  355.4 8.2 slice-start.6
  355.4 8.2 slice-start.7
  374.1 319.6 %reduce-scatter.14.cloned.1.call-start = ((), (), s32[]{:S(2)}) async-start(), calls=%async_computation.11 | async-start | bytes 9732096 | tf_op jit(solution)/shard_map/reduce_scatter | solution.py:40
  392.1 443.7 %reduce-scatter.12.cloned.1.call-start = ((), (), s32[]{:S(2)}) async-start(), calls=%async_computation.10 | async-start | bytes 9732096 | tf_op jit(solution)/shard_map/reduce_scatter | solution.py:39
  469.9 10.0 %copy-start.26 = (bf16[1024,768]{1,0:T(8,128)(2,1)S(1)}, bf16[1024,768]{1,0:T(8,128)(2,1)}, u32[]{:S(2)}) copy-start(bf16[1024,768]{1,0:T(8,128)(2,1)} %param.23) | copy-start | bytes 4718596
  469.9 10.0 %copy-start.28 = (f32[512,768]{1,0:T(8,128)S(1)}, f32[512,768]{1,0:T(8,128)}, u32[]{:S(2)}) copy-start(f32[512,768]{1,0:T(8,128)} %copy-done.27) | copy-start | bytes 4718596
  469.9 9.9 %copy-start.30 = (f32[512,768]{1,0:T(8,128)S(1)}, f32[512,768]{1,0:T(8,128)}, u32[]{:S(2)}) copy-start(f32[512,768]{1,0:T(8,128)} %copy-done.29) | copy-start | bytes 4718596
  (79 other events, 216.8 us)
Sparse Core Ops, SparseCore 0:
  11.0 62.8 all-gather.7
  76.8 52.7 all-gather.9
  132.5 62.5 all-gather.11
  197.8 62.3 all-gather.13
  329.2 97.8 reduce-scatter.9
  434.1 118.1 reduce-scatter.7
  558.8 134.8 reduce-scatter.13
  701.2 134.5 reduce-scatter.11
where the time goes:
time: 847 us; the launch traced here: 843 us
  waiting for transfers between devices  374 us (44%)
  blocking collectives  198 us (23%)
  matrix products  181 us (21%)
  other arithmetic  40.7 us (5%)
  local copies, waits for them, and re-layouts  33.7 us (4%)
  between operations  16 us (2%)
    reduce_scatter x1, waiting for transfers between devices, settle(): lax.psum_scatter(up_sum, ('fsdp', 'rep'), scatter_dimension=0, tiled=True)  142 us
    reduce_scatter x1, waiting for transfers between devices, settle(): lax.psum_scatter(down_sum, ('fsdp', 'rep'), scatter_dimension=0, tiled=True)  141 us
    unnamed x2, blocking collectives  82.9 us
    reduce_scatter x1, waiting for transfers between devices, settle(): lax.psum_scatter(qkv_sum, ('fsdp', 'rep'), scatter_dimension=0, tiled=True)  68.5 us
    all_gather x1, blocking collectives, fetch(): lax.all_gather(ln_gain, ('fsdp', 'rep'), axis=1, tiled=True)  40.2 us
    all_gather x1, blocking collectives, fetch(): lax.all_gather(bias_attn, ('fsdp', 'rep'), axis=1, tiled=True)  38.2 us
    all_gather x1, blocking collectives, fetch(): lax.all_gather(ln_bias, ('fsdp', 'rep'), axis=1, tiled=True)  36.4 us
    dot_general x2, matrix products, backward_block(): jnp.einsum('qhd,khd->hqk', grad_att, values, preferred_element_type=jnp.f...  27.5 us
  transfers between devices with their start and end apart: 8, of which 4 were waited for; matrix products, arithmetic and copies ran while one was open for 21% of the time, Pallas kernels for 0%

commit v1 on v0

v1 whole, which is shorter than its diff:
```python
import functools
import jax
import jax.numpy as jnp
from jax import lax
from jax.experimental import pallas as pl
from jax.experimental.pallas import tpu as pltpu
from jax.sharding import PartitionSpec as P

HEAD = 64
PAIR = 128
REACH = 256
EPSILON = 1e-05
SCORE_SCALE = 0.125
MASK_VALUE = -1000000000.0
AXES = ("fsdp", "rep")
MESH = pl.DeviceIdType.MESH
MIB = 1 << 20


def bits_of(sizes):
    out = []
    for axis, size in zip(AXES, sizes):
        weight = size // 2
        while weight:
            out.append((axis, weight))
            weight //= 2
    return out


def powers(sizes):
    return all(size & (size - 1) == 0 for size in sizes)


def orders_of(count):
    near = count - 1
    rest = list(range(near))
    if count == 5:
        base = [[0, 1, 2, 3], [3, 0, 1, 2], [2, 3, 0, 1]]
    else:
        third = max(1, len(rest) // 3)
        base = [rest[k * third :] + rest[: k * third] for k in range(3)]
    return [order + [near] for order in base]


def position(bits):
    place = {axis: lax.axis_index(axis) for axis in AXES}
    mine = [lax.rem(place[axis] // weight, 2) for axis, weight in bits]
    partners = []
    for (axis, weight), own in zip(bits, mine):
        there = dict(place)
        there[axis] = place[axis] + weight * (1 - 2 * own)
        partners.append(tuple(there[a] for a in AXES))
    return mine, partners


def greet(partners):
    barrier = pltpu.get_barrier_semaphore()
    for partner in partners:
        pl.semaphore_signal(barrier, inc=1, device_id=partner, device_id_type=MESH)
    pl.semaphore_wait(barrier, len(partners))


def parts_of(widths):
    pieces = []
    for tensor, width in enumerate(widths):
        if width % (3 * 128):
            pieces.append((tensor, 0, 0, width))
        else:
            third = width // 3
            pieces += [(tensor, k, k * third, third) for k in range(3)]
    return pieces


def gather_kernel(bits, pieces, count, *refs):
    shards, wholes = refs[:count], refs[count : 2 * count]
    send_sems, recv_sems, own_sems = refs[2 * count :]
    depth = len(bits)
    orders = orders_of(depth)
    mine, partners = position(bits)
    own = [
        pltpu.make_async_copy(shards[t], wholes[t].at[tuple(mine)], own_sems.at[t])
        for t in range(count)
    ]
    for copy in own:
        copy.start()
    greet(partners)
    for copy in own:
        copy.wait()

    def step(number, stage):
        tensor, order, first, columns = pieces[number]
        sequence = orders[order]
        done = sequence[:stage]
        where = tuple(slice(None) if k in done else mine[k] for k in range(depth))
        block = wholes[tensor].at[where + (slice(None), pl.ds(first, columns))]
        return pltpu.make_async_remote_copy(
            src_ref=block,
            dst_ref=block,
            send_sem=send_sems.at[number, stage],
            recv_sem=recv_sems.at[number, stage],
            device_id=partners[sequence[stage]],
            device_id_type=MESH,
        )

    for number in range(len(pieces)):
        step(number, 0).start()
    for stage in range(1, depth):
        for number in range(len(pieces)):
            step(number, stage - 1).wait_recv()
            step(number, stage).start()
    for number in range(len(pieces)):
        step(number, depth - 1).wait_recv()
    for stage in range(depth):
        for number in range(len(pieces)):
            step(number, stage).wait_send()


def gather_all(shards, sizes, collective_id):
    bits = bits_of(sizes)
    depth = len(bits)
    pieces = parts_of([shard.shape[1] for shard in shards])
    count = len(shards)
    total = sum(shard.size * shard.dtype.itemsize for shard in shards)
    wholes = pl.pallas_call(
        functools.partial(gather_kernel, bits, pieces, count),
        out_shape=[jax.ShapeDtypeStruct((2,) * depth + s.shape, s.dtype) for s in shards],
        in_specs=[pl.BlockSpec(memory_space=pl.ANY)] * count,
        out_specs=[pl.BlockSpec(memory_space=pl.ANY)] * count,
        scratch_shapes=[
            pltpu.SemaphoreType.DMA((len(pieces), depth)),
            pltpu.SemaphoreType.DMA((len(pieces), depth)),
            pltpu.SemaphoreType.DMA((count,)),
        ],
        compiler_params=pltpu.CompilerParams(collective_id=collective_id, has_side_effects=True),
        cost_estimate=pl.CostEstimate(
            flops=0, bytes_accessed=total << (depth + 1), transcendentals=0
        ),
    )(*shards)
    return [w.reshape((-1,) + w.shape[depth + 1 :]) for w in wholes]


def scatter_kernel(bits, pieces, count, *refs):
    parts, sums = refs[:count], refs[count : 2 * count]
    depth = len(bits)
    number_of = len(pieces)
    lands = refs[2 * count : 2 * count + number_of * depth]
    send_sems, recv_sems = refs[2 * count + number_of * depth :]
    orders = [list(reversed(order)) for order in orders_of(depth)]
    mine, partners = position(bits)
    greet(partners)

    def left_after(order, stage):
        gone = orders[order][:stage]
        return [k for k in range(depth) if k not in gone]

    def half(number, stage, whose, rest):
        tensor, order, first, columns = pieces[number]
        bit = orders[order][stage]
        side = mine[bit] if whose else 1 - mine[bit]
        index, rest = [], list(rest)
        for k in left_after(order, stage):
            index.append(side if k == bit else rest.pop(0))
        if stage == 0:
            return parts[tensor], tuple(index) + (slice(None), pl.ds(first, columns))
        return lands[number * depth + stage - 1], tuple(index)

    def step(number, stage):
        tensor, order, first, columns = pieces[number]
        buffer, index = half(number, stage, False, [slice(None)] * (depth - 1 - stage))
        return pltpu.make_async_remote_copy(
            src_ref=buffer.at[index],
            dst_ref=lands[number * depth + stage],
            send_sem=send_sems.at[number, stage],
            recv_sem=recv_sems.at[number, stage],
            device_id=partners[orders[order][stage]],
            device_id_type=MESH,
        )

    def settle(number, stage):
        tensor, order, first, columns = pieces[number]
        land = lands[number * depth + stage]
        free = depth - 1 - stage

        def one(i, carry):
            rest = [lax.rem(i // (1 << (free - 1 - k)), 2) for k in range(free)]
            buffer, index = half(number, stage, True, rest)
            value = buffer[index].astype(jnp.float32) + land[tuple(rest)].astype(jnp.float32)
            land[tuple(rest)] = value.astype(land.dtype)
            return carry

        if free:
            lax.fori_loop(0, 1 << free, one, 0)
        else:
            buffer, index = half(number, stage, True, [])
            value = buffer[index].astype(jnp.float32) + land[...].astype(jnp.float32)
            sums[tensor][:, pl.ds(first, columns)] = value

    for number in range(number_of):
        step(number, 0).start()
    for stage in range(depth):
        for number in range(number_of):
            step(number, stage).wait_recv()
            settle(number, stage)
            if stage + 1 < depth:
                step(number, stage + 1).start()
    for stage in range(depth):
        for number in range(number_of):
            step(number, stage).wait_send()


def scatter_all(totals, sizes, collective_id):
    bits = bits_of(sizes)
    depth = len(bits)
    devices = 1 << depth
    count = len(totals)
    parts = [
        t.reshape((2,) * depth + (t.shape[0] // devices, t.shape[1])) for t in totals
    ]
    pieces = parts_of([t.shape[1] for t in totals])
    lands = []
    for tensor, order, first, columns in pieces:
        rows = parts[tensor].shape[depth]
        for stage in range(depth):
            lands.append(
                pltpu.VMEM((2,) * (depth - 1 - stage) + (rows, columns), parts[tensor].dtype)
            )
    moved = sum(t.size * t.dtype.itemsize for t in totals)
    return pl.pallas_call(
        functools.partial(scatter_kernel, bits, pieces, count),
        out_shape=[
            jax.ShapeDtypeStruct((t.shape[0] // devices, t.shape[1]), jnp.float32) for t in totals
        ],
        in_specs=[pl.BlockSpec(memory_space=pltpu.VMEM)] * count,
        out_specs=[pl.BlockSpec(memory_space=pltpu.VMEM)] * count,
        scratch_shapes=lands
        + [
            pltpu.SemaphoreType.DMA((len(pieces), depth)),
            pltpu.SemaphoreType.DMA((len(pieces), depth)),
        ],
        compiler_params=pltpu.CompilerParams(
            collective_id=collective_id, has_side_effects=True, vmem_limit_bytes=56 * MIB
        ),
        cost_estimate=pl.CostEstimate(flops=0, bytes_accessed=2 * moved, transcendentals=0),
    )(*parts)


def dot_nt(left, right):
    return lax.dot_general(
        left, right, (((1,), (1,)), ((), ())), preferred_element_type=jnp.float32
    )


def dot_tn(left, right):
    return lax.dot_general(
        left, right, (((0,), (0,)), ((), ())), preferred_element_type=jnp.float32
    )


def windows(length):
    step = PAIR if length % PAIR == 0 else length
    for row in range(0, length, step):
        yield row, step, max(0, row - (REACH if step == PAIR else length)), row + step


def masks_of(seg_row_ref, seg_col_ref, row, step, low, high):
    places = row + lax.broadcasted_iota(jnp.int32, (step, high - low), 0)
    others = low + lax.broadcasted_iota(jnp.int32, (step, high - low), 1)
    same = seg_col_ref[0, row : row + step, :] == seg_row_ref[0, :, low:high]
    return same & (others <= places)


def first_half(shape):
    return lax.broadcasted_iota(jnp.int32, shape, 1) < HEAD


def attention_kernel(joined_ref, seg_row_ref, seg_col_ref, att_ref, norm_ref):
    length = joined_ref.shape[0]
    width = att_ref.shape[1]
    for row, step, low, high in windows(length):
        allowed = masks_of(seg_row_ref, seg_col_ref, row, step, low, high)

        def pair(number, carry):
            at = pl.multiple_of(number * PAIR, PAIR)
            queries = joined_ref[row : row + step, pl.ds(at, PAIR)] * SCORE_SCALE
            keys = joined_ref[low:high, pl.ds(width + at, PAIR)]
            values = joined_ref[low:high, pl.ds(2 * width + at, PAIR)]
            left = first_half((step, PAIR))
            outs, norms = [], []
            for lanes in (left, ~left):
                scores = dot_nt(jnp.where(lanes, queries, 0).astype(jnp.bfloat16), keys)
                scores = jnp.where(allowed, scores, MASK_VALUE)
                top = jnp.max(scores, axis=-1, keepdims=True)
                weights = jnp.exp(scores - top)
                total = jnp.sum(weights, axis=-1, keepdims=True)
                probs = (weights * (1.0 / total)).astype(jnp.bfloat16)
                outs.append(jnp.dot(probs, values, preferred_element_type=jnp.float32))
                norms.append(jnp.broadcast_to(top + jnp.log(total), (step, PAIR)))
            att_ref[row : row + step, pl.ds(at, PAIR)] = jnp.where(left, *outs).astype(
                jnp.bfloat16
            )
            norm_ref[row : row + step, pl.ds(at, PAIR)] = jnp.where(left, *norms)
            return carry

        lax.fori_loop(0, width // PAIR, pair, 0)


def attention_back_kernel(
    joined_ref, grad_ref, norm_ref, seg_row_ref, seg_col_ref, out_ref, keys_sum, values_sum
):
    length, width = grad_ref.shape
    keys_sum[...] = jnp.zeros_like(keys_sum)
    values_sum[...] = jnp.zeros_like(values_sum)
    for row, step, low, high in windows(length):
        allowed = masks_of(seg_row_ref, seg_col_ref, row, step, low, high)

        def pair(number, carry):
            at = pl.multiple_of(number * PAIR, PAIR)
            queries = joined_ref[row : row + step, pl.ds(at, PAIR)]
            keys = joined_ref[low:high, pl.ds(width + at, PAIR)]
            values = joined_ref[low:high, pl.ds(2 * width + at, PAIR)]
            grads = grad_ref[row : row + step, pl.ds(at, PAIR)]
            norms = norm_ref[row : row + step, pl.ds(at, PAIR)]
            scaled = queries * SCORE_SCALE
            left = first_half((step, PAIR))
            tall = first_half((high - low, PAIR))
            d_query, d_keys, d_values = [], [], []
            for lanes, lane in ((left, 0), (~left, HEAD)):
                scores = dot_nt(jnp.where(lanes, scaled, 0).astype(jnp.bfloat16), keys)
                probs = jnp.where(allowed, jnp.exp(scores - norms[:, lane : lane + 1]), 0.0)
                d_probs = dot_nt(jnp.where(lanes, grads, 0).astype(jnp.bfloat16), values)
                inner = jnp.sum(probs * d_probs, axis=-1, keepdims=True)
                d_scores = (probs * (d_probs - inner)).astype(jnp.bfloat16)
                d_query.append(jnp.dot(d_scores, keys, preferred_element_type=jnp.float32))
                d_keys.append(dot_tn(d_scores, queries))
                d_values.append(dot_tn(probs.astype(jnp.bfloat16), grads))
            out_ref[row : row + step, pl.ds(at, PAIR)] = (
                jnp.where(left, *d_query) * SCORE_SCALE
            ).astype(jnp.bfloat16)
            keys_sum[low:high, pl.ds(at, PAIR)] += jnp.where(tall, *d_keys)
            values_sum[low:high, pl.ds(at, PAIR)] += jnp.where(tall, *d_values)
            return carry

        lax.fori_loop(0, width // PAIR, pair, 0)
    out_ref[:, width : 2 * width] = (keys_sum[...] * SCORE_SCALE).astype(jnp.bfloat16)
    out_ref[:, 2 * width :] = values_sum[...].astype(jnp.bfloat16)


def seg_views(seg_ids):
    batches, length = seg_ids.shape
    return seg_ids.reshape(batches, 1, length), seg_ids.reshape(batches, length, 1)


def row_spec(length, width):
    return pl.BlockSpec((length, width), lambda b: (b, 0))


def seg_specs(length):
    return [
        pl.BlockSpec((1, 1, length), lambda b: (b, 0, 0)),
        pl.BlockSpec((1, length, 1), lambda b: (b, 0, 0)),
    ]


def attention(joined, seg_ids):
    batches, length = seg_ids.shape
    rows = joined.shape[0]
    width = joined.shape[1] // 3
    return pl.pallas_call(
        attention_kernel,
        grid=(batches,),
        in_specs=[row_spec(length, 3 * width)] + seg_specs(length),
        out_specs=[row_spec(length, width), row_spec(length, width)],
        out_shape=[
            jax.ShapeDtypeStruct((rows, width), jnp.bfloat16),
            jax.ShapeDtypeStruct((rows, width), jnp.float32),
        ],
        compiler_params=pltpu.CompilerParams(vmem_limit_bytes=40 * MIB),
    )(joined, *seg_views(seg_ids))


def attention_back(joined, grad_att, norms, seg_ids):
    batches, length = seg_ids.shape
    rows, width = grad_att.shape
    return pl.pallas_call(
        attention_back_kernel,
        grid=(batches,),
        in_specs=[row_spec(length, 3 * width), row_spec(length, width), row_spec(length, width)]
        + seg_specs(length),
        out_specs=row_spec(length, 3 * width),
        out_shape=jax.ShapeDtypeStruct((rows, 3 * width), jnp.bfloat16),
        scratch_shapes=[
            pltpu.VMEM((length, width), jnp.float32),
            pltpu.VMEM((length, width), jnp.float32),
        ],
        compiler_params=pltpu.CompilerParams(vmem_limit_bytes=40 * MIB),
    )(joined, grad_att, norms, *seg_views(seg_ids))


def norm_rows(inputs, scaling, offset):
    row_mean = jnp.mean(inputs, axis=-1, keepdims=True)
    centred = inputs - row_mean
    spread = jnp.mean(centred * centred, axis=-1, keepdims=True)
    return centred * lax.rsqrt(spread + EPSILON) * scaling + offset


def pack_small(gain, shift, attn, up, down):
    width = -(-max(gain.shape[1], up.shape[0] + down.shape[0]) // 128) * 128
    rows = jnp.concatenate([gain, shift, attn], axis=0).astype(jnp.float32)
    last = jnp.concatenate([up, down]).astype(jnp.float32)
    return jnp.concatenate(
        [
            jnp.pad(rows, ((0, 0), (0, width - rows.shape[1]))),
            jnp.pad(last, (0, width - last.shape[0]))[None],
        ],
        axis=0,
    )


def fetch(w_qkv, w_out, w_up, w_down, small, sizes):
    devices = sizes[0] * sizes[1]
    if powers(sizes) and w_qkv.shape[0] % 8 == 0:
        wholes = gather_all([w_qkv, w_out, w_up, w_down, small], sizes, 1)
    else:
        wholes = [
            lax.all_gather(w, AXES, axis=0, tiled=True)
            for w in (w_qkv, w_out, w_up, w_down, small)
        ]
    return wholes[:4], wholes[4].reshape(devices, small.shape[0], small.shape[1])


def settle_all(totals, small, sizes):
    flat = small.reshape(-1, small.shape[2])
    devices = sizes[0] * sizes[1]
    if powers(sizes) and (totals[0].shape[0] // devices) % 8 == 0:
        sums = scatter_all(list(totals) + [flat], sizes, 2)
    else:
        sums = [
            lax.psum_scatter(
                t.astype(jnp.float32), AXES, scatter_dimension=0, tiled=True
            )
            for t in list(totals) + [flat]
        ]
    return sums[:4], sums[4]


def local(
    sizes,
    tokens,
    seg_ids,
    w_qkv,
    w_out,
    w_up,
    w_down,
    ln_gain,
    ln_bias,
    bias_attn,
    bias_up,
    bias_down,
    grad_out,
):
    devices = sizes[0] * sizes[1]
    model_width = tokens.shape[1]
    own = ln_gain.shape[1]
    own_up = bias_up.shape[0]
    (w_qkv, w_out, w_up, w_down), small = fetch(
        w_qkv,
        w_out,
        w_up,
        w_down,
        pack_small(ln_gain, ln_bias, bias_attn, bias_up, bias_down),
        sizes,
    )
    features = jnp.swapaxes(small[:, :7, :own], 0, 1).reshape(7, devices * own)
    gains, shifts, attn_bias = features[0:2], features[2:4], features[4:7]
    up_bias = small[:, 7, :own_up].reshape(-1)
    down_bias = small[:, 7, own_up : own_up + own].reshape(-1)

    rows_float = tokens.astype(jnp.float32)
    normed, norm_one = jax.vjp(norm_rows, rows_float, gains[0], shifts[0])
    normed_low = normed.astype(jnp.bfloat16)
    zero_bias = jnp.zeros((model_width,), jnp.float32)
    qkv_bias = jnp.concatenate([attn_bias[0], zero_bias, attn_bias[1]])
    joined = (jnp.dot(normed_low, w_qkv, preferred_element_type=jnp.float32) + qkv_bias).astype(
        jnp.bfloat16
    )
    attended, norms = attention(joined, seg_ids)
    residual = (
        rows_float + jnp.dot(attended, w_out, preferred_element_type=jnp.float32) + attn_bias[2]
    )
    second, norm_two = jax.vjp(norm_rows, residual, gains[1], shifts[1])
    second_low = second.astype(jnp.bfloat16)
    pre_act = jnp.dot(second_low, w_up, preferred_element_type=jnp.float32) + up_bias
    active, gelu_back = jax.vjp(jax.nn.gelu, pre_act)
    active_low = active.astype(jnp.bfloat16)
    layer_out = (
        residual + jnp.dot(active_low, w_down, preferred_element_type=jnp.float32) + down_bias
    ).astype(jnp.bfloat16)

    grad_float = grad_out.astype(jnp.float32)
    down_sum = dot_tn(active_low, grad_out).astype(jnp.bfloat16)
    downb_sum = jnp.sum(grad_float, axis=0)
    grad_active = dot_nt(grad_out, w_down)
    grad_pre = gelu_back(grad_active)[0].astype(jnp.bfloat16)
    up_sum = dot_tn(second_low, grad_pre).astype(jnp.bfloat16)
    upb_sum = jnp.sum(grad_pre.astype(jnp.float32), axis=0)
    grad_second = dot_nt(grad_pre, w_up)
    grad_resid, gain_two, shift_two = norm_two(grad_second)
    grad_resid = grad_resid + grad_float
    grad_resid_low = grad_resid.astype(jnp.bfloat16)
    out_sum = dot_tn(attended, grad_resid_low).astype(jnp.bfloat16)
    bias_out_grad = jnp.sum(grad_resid_low.astype(jnp.float32), axis=0)
    grad_att = dot_nt(grad_resid_low, w_out).astype(jnp.bfloat16)
    grad_joined = attention_back(joined, grad_att, norms, seg_ids)
    qkv_sum = dot_tn(normed_low, grad_joined).astype(jnp.bfloat16)
    joined_bias = jnp.sum(grad_joined.astype(jnp.float32), axis=0)
    grad_normed = dot_nt(grad_joined, w_qkv)
    grad_input, gain_one, shift_one = norm_one(grad_normed)
    grad_tokens = (grad_resid + grad_input).astype(jnp.bfloat16)

    features = jnp.stack(
        [
            gain_one,
            gain_two,
            shift_one,
            shift_two,
            joined_bias[:model_width],
            joined_bias[2 * model_width :],
            bias_out_grad,
        ]
    )
    features = jnp.swapaxes(features.reshape(7, devices, own), 0, 1)
    last = jnp.concatenate(
        [upb_sum.reshape(devices, own_up), downb_sum.reshape(devices, own)], axis=1
    )
    width = small.shape[2]
    packed = jnp.concatenate(
        [
            jnp.pad(features, ((0, 0), (0, 0), (0, width - own))),
            jnp.pad(last, ((0, 0), (0, width - last.shape[1])))[:, None],
        ],
        axis=1,
    )
    sums, packed = settle_all([qkv_sum, out_sum, up_sum, down_sum], packed, sizes)
    return (
        layer_out,
        grad_tokens,
        *sums,
        packed[0:2, :own],
        packed[2:4, :own],
        packed[4:7, :own],
        packed[7, :own_up],
        packed[7, own_up : own_up + own],
    )


def solution(mesh):
    return jax.shard_map(
        functools.partial(local, (mesh.shape["fsdp"], mesh.shape["rep"])),
        mesh=mesh,
        in_specs=(
            P(("fsdp", "rep"), None),
            P(("fsdp", "rep"), None),
            P(("fsdp", "rep"), None),
            P(("fsdp", "rep"), None),
            P(("fsdp", "rep"), None),
            P(("fsdp", "rep"), None),
            P(None, ("fsdp", "rep")),
            P(None, ("fsdp", "rep")),
            P(None, ("fsdp", "rep")),
            P(("fsdp", "rep")),
            P(("fsdp", "rep")),
            P(("fsdp", "rep"), None),
        ),
        out_specs=(
            P(("fsdp", "rep"), None),
            P(("fsdp", "rep"), None),
            P(("fsdp", "rep"), None),
            P(("fsdp", "rep"), None),
            P(("fsdp", "rep"), None),
            P(("fsdp", "rep"), None),
            P(None, ("fsdp", "rep")),
            P(None, ("fsdp", "rep")),
            P(None, ("fsdp", "rep")),
            P(("fsdp", "rep")),
            P(("fsdp", "rep")),
        ),
        check_vma=False,
    )
```

time: 847 us -> 421 us (0.50)
  waiting for transfers between devices: 374 us -> 0 us
  Pallas kernels: 0 us -> 259 us
  blocking collectives: 198 us -> 0 us
  matrix products: 181 us -> 96.1 us
  other arithmetic: 40.7 us -> 22.2 us
  between operations: 16 us -> 1.7 us
    reduce_scatter x4 -> x0, waiting for transfers between devices: 352 us -> none  [the longest x1 142 us: settle(): lax.psum_scatter(up_sum, ('fsdp', 'rep'), scatter_dimension=0, tiled=True)]
    pallas_call x0 -> x4, Pallas kernels: none -> 259 us  [the longest x1 91.8 us: gather_all(): pl.pallas_call(functools.partial(gather_kernel, bits, pieces, count), out...]
    all_gather x3 -> x0, blocking collectives: 115 us -> none  [the longest x1 40.2 us: fetch(): lax.all_gather(ln_gain, ('fsdp', 'rep'), axis=1, tiled=True)]
    dot_general x36 -> x12, matrix products: 181 us -> 96.1 us  [the longest x4 34.3 us: dot_nt(): lax.dot_general(left, right, (((1,), (1,)), ((), ())), preferred_element_...]
    unnamed x2 -> x0, blocking collectives: 82.9 us -> none
    convert_element_type x7 -> x0, other arithmetic: 20.1 us -> none  [the longest x2 14.8 us: backward_block(): grad_scores = grad_scores.astype(jnp.bfloat16)]
    all_gather x4 -> x0, waiting for transfers between devices: 19.2 us -> none  [the longest x1 19.1 us: fetch(): lax.all_gather(w_down, ('fsdp', 'rep'), axis=0, tiled=True)]
    slice x11 -> x6, local copies, waits for them, and re-layouts: 15.2 us -> 4.55 us  [the longest x1 1.32 us: local(): packed[2:4, :own]]
  transfers between devices with their start and end apart: 8 -> 0, of which waited for: 4 -> 0; matrix products, arithmetic and copies ran while one was open for 21% -> 0% of each run, Pallas kernels for 0% -> 0%
where the time goes in v1:
time: 421 us; the launch traced here: 413 us
  Pallas kernels  259 us (62%)
  matrix products  96.1 us (23%)
  local copies, waits for them, and re-layouts  33.9 us (8%)
  other arithmetic  22.2 us (5%)
    pallas_call x1, Pallas kernels, gather_all(): pl.pallas_call(functools.partial(gather_kernel, bits, pieces, count), out...  91.8 us
    pallas_call x1, Pallas kernels, scatter_all(): pl.pallas_call(functools.partial(scatter_kernel, bits, pieces, count), ou...  83.9 us
    pallas_call x1, Pallas kernels, attention_back(): pl.pallas_call(attention_back_kernel, grid=(batches,), in_specs=[row_spec...  43.7 us
    pallas_call x1, Pallas kernels, attention(): pl.pallas_call(attention_kernel, grid=(batches,), in_specs=[row_spec(leng...  39.5 us
    dot_general x4, matrix products, dot_nt(): lax.dot_general(left, right, (((1,), (1,)), ((), ())), preferred_element_...  34.3 us
    dot_general x4, matrix products, dot_tn(): lax.dot_general(left, right, (((0,), (0,)), ((), ())), preferred_element_...  32.8 us
    unnamed x66, local copies, waits for them, and re-layouts  16.3 us
    dot_general x1, matrix products, local(): jnp.dot(active_low, w_down, preferred_element_type=jnp.float32)  12.3 us

profile of v1, /device:TPU:0, one launch (start us, length us, event | category | flops | bytes accessed | tf_op | source)
XLA Modules:
  0.0 412.9 jit_solution(1671576172271275791)
XLA Ops:
  0.6 0.7 fusion.32
  1.4 0.7 fusion.30
  2.1 0.6 maximum_convert_fusion.refs_4_
  2.7 0.7 reshape.172.seg_row_ref
  3.4 0.9 copy.34.seg_col_ref
  4.3 1.7 copy.32
  6.8 2.6 copy.38
  9.4 91.8 %shard_map.203 = (bf16[2,2,2,2,2,24,2304]{6,5,4,3,2,1,0:T(8,128)(2,1)}, bf16[2,2,2,2,2,24,768]{6,5,4,3,2,1,0:T(8,128)(2,1)}, bf16[2,2,2,2,2,24,3072]{6,5,4,3,2,1...) custom-call(bf16[24,2304]{1,0:T(8,128)(2,1)} %refs_0_.1, ...), custom_call_target="tpu_custom_call" | custom-call | bytes 28573696 | tf_op jit(solution)/shard_map/pallas_call | solution.py:124
  101.3 1.0 slice_reduce_fusion
  102.3 1.0 slice.109
  103.4 0.9 copy.51
  105.0 6.4 %add_convert_fusion.joined_ref = bf16[1024,2304]{1,0:T(8,128)(2,1)S(1)} fusion(bf16[768,2304]{1,0:T(8,128)(2,1)} %bitcast.76, f32[2304]{0:T(1024)S(1)} %pad_maximum_fusion.1, bf16[1024,768]{0,1:T(8,128)(2,1)S(1)} %copy.32, f32[768]{0:T(1024)S(1)} %add.106, f32[768]{0:T(1024)S(1)} %mul.157, f32[1024]{0:T(1024)S(1)} %fusion.27, ...), kind=kOutput, calls=%fused_computation.17 | convolution fusion | flops 3633315840 | bytes 9853952 | tf_op jit(solution)/shard_map/dot_general | solution.py:483
  111.4 39.5 %shard_map.204 = (bf16[1024,768]{1,0:T(8,128)(2,1)S(1)}, f32[1024,768]{1,0:T(8,128)S(1)}) custom-call(bf16[1024,2304]{1,0:T(8,128)(2,1)S(1)} %add_convert_fusion.joined_ref, s32[2,1,512]{2,1,0:T(1,128)S(1)} %reshape.172.seg_row_ref, s32[2,512,1]{2,1,0:T(8,128)S(1)} %copy.34.seg_col_ref), custom_call_target="tpu_custom_call" | custom-call | tf_op jit(solution)/shard_map/pallas_call | solution.py:368
  151.0 1.7 fusion.41
  153.1 2.3 slice-done
  155.5 8.6 %fusion.35 = f32[1024,3072]{1,0:T(8,128)} fusion(bf16[768,3072]{1,0:T(8,128)(2,1)S(1)} %bitcast.62, f32[1024,768]{0,1:T(8,128)S(1)} %get-tuple-element.79, f32[768]{0:T(1024)S(1)} %add.116, f32[768]{0:T(1024)S(1)} %mul.163, f32[1024]{0:T(1024)S(1)} %fusion.28, f32[1024]{0:T(1024)S(1)} %broadcast_multiply_fusion), kind=kOutput, calls=%fused_computation.87 | convolution fusion | flops 4835770368 | bytes 20461568 | tf_op jit(solution)/shard_map/dot_general | solution.py:492
  164.1 12.3 %add_convert_fusion.2 = bf16[1024,768]{0,1:T(8,128)(2,1)} fusion(f32[1024,768]{0,1:T(8,128)S(1)} %get-tuple-element.79, bf16[3072,768]{1,0:T(8,128)(2,1)} %bitcast.74, f32[768]{0:T(1024)S(1)} %add.125, f32[1024,3072]{1,0:T(8,128)} %fusion.35, f32[3072]{0:T(1024)S(1)} %add.119), kind=kOutput, calls=%fused_computation.44 | convolution fusion | flops 4865654784 | bytes 22035456 | tf_op jit(solution)/shard_map/dot_general | solution.py:496
  176.4 2.6 copy.44
  179.0 16.3 %convert_reduce_fusion = (f32[3072]{0:T(1024)S(1)}, bf16[1024,3072]{1,0:T(8,128)(2,1)S(1)}) fusion(f32[1024,3072]{1,0:T(8,128)} %fusion.35, f32[3072]{0:T(1024)S(1)} %add.119, bf16[3072,768]{1,0:T(8,128)(2,1)} %bitcast.75, bf16[1024,768]{1,0:T(8,128)(2,1)} %param.23), kind=kOutput, calls=%fused_computation.14 | convolution fusion | flops 4904186880 | bytes 25190400 | tf_op jit(solution)/shard_map/dot_general | solution.py:248
  195.3 14.5 %convolution_convert_fusion = bf16[3072,768]{1,0:T(8,128)(2,1)} fusion(bf16[1024,768]{1,0:T(8,128)(2,1)S(1)} %copy-done.14, f32[1024,3072]{1,0:T(8,128)} %fusion.35, f32[3072]{0:T(1024)S(1)} %add.119), kind=kOutput, calls=%fused_computation.18 | convolution fusion | flops 4865654784 | bytes 18886656 | tf_op jit(solution)/shard_map/dot_general | solution.py:254
  209.9 9.1 %fusion.43 = (f32[768]{0:T(1024)S(1)}, f32[1024,768]{1,0:T(8,128)}) fusion(bf16[1024,3072]{1,0:T(8,128)(2,1)S(1)} %get-tuple-element.81, bf16[768,3072]{1,0:T(8,128)(2,1)} %bitcast.59), kind=kOutput, calls=%fused_computation.94 | convolution fusion | flops 4832623616 | bytes 14158848 | tf_op jit(solution)/shard_map/dot_general | solution.py:248
  219.1 3.6 copy.37
  222.7 3.9 multiply_reduce_fusion
  226.7 10.1 %convolution_convert_fusion.1 = bf16[768,3072]{1,0:T(8,128)(2,1)} fusion(bf16[1024,3072]{1,0:T(8,128)(2,1)} %copy-done.22, f32[1024,768]{0,1:T(8,128)S(1)} %copy-done.9, f32[768]{0:T(1024)S(1)} %add.116, f32[768]{0:T(1024)S(1)} %mul.163, f32[1024]{0:T(1024)S(1)} %fusion.28, f32[1024]{0:T(1024)S(1)} %broadcast_multiply_fusion), kind=kOutput, calls=%fused_computation.19 | convolution fusion | flops 4838129664 | bytes 14170112 | tf_op jit(solution)/shard_map/dot_general | solution.py:254
  236.8 2.6 fusion.37
  239.4 2.9 convert_reduce_fusion.4
  242.4 2.5 convolution_convert_fusion.4
  244.9 3.3 convolution_convert_fusion.3.grad_ref
  248.3 43.7 %shard_map.205 = bf16[1024,2304]{1,0:T(8,128)(2,1)S(1)} custom-call(bf16[1024,2304]{1,0:T(8,128)(2,1)} %copy-done, bf16[1024,768]{1,0:T(8,128)(2,1)S(1)} %convolution_convert_fusion.3.grad_ref, f32[1024,768]{1,0:T(8,128)S(1)} %copy-done.4, s32[2,1,512]{2,1,0:T(1,128)S(1)} %reshape.172.seg_row_ref, s32[2,512,1]{2,1,0:T(8,128)S(1)} %copy.34.seg_col_ref), custom_call_target="tpu_custom_call" | custom-call | tf_op jit(solution)/shard_map/pallas_call | solution.py:384
  292.0 5.6 %fusion.42 = (f32[768]{0:T(1024)S(1)}, f32[1024,768]{1,0:T(8,128)}) fusion(bf16[1024,2304]{1,0:T(8,128)(2,1)S(1)} %shard_map.205, bf16[768,2304]{1,0:T(8,128)(2,1)S(1)} %bitcast.77), kind=kOutput, calls=%fused_computation.93 | convolution fusion | flops 3624664320 | bytes 11406336 | tf_op jit(solution)/shard_map/dot_general | solution.py:248
  297.7 3.2 convert_reduce_fusion.1
  300.9 0.6 copy-done.2
  301.4 5.7 %convolution_convert_fusion.2 = bf16[768,2304]{1,0:T(8,128)(2,1)} fusion(bf16[1024,2304]{1,0:T(8,128)(2,1)S(1)} %copy-done.2, bf16[1024,768]{0,1:T(8,128)(2,1)S(1)} %copy-done.7, f32[768]{0:T(1024)S(1)} %add.106, f32[768]{0:T(1024)S(1)} %mul.157, f32[1024]{0:T(1024)S(1)} %fusion.27, f32[1024]{0:T(1024)S(1)} %broadcast_multiply_fusion.1), kind=kOutput, calls=%fused_computation.20 | convolution fusion | flops 3630366720 | bytes 9844736 | tf_op jit(solution)/shard_map/dot_general | solution.py:254
  307.3 3.9 copy.40
  311.2 2.6 fusion.20
  314.0 1.3 fusion.18
  316.2 1.7 convert_reduce_fusion.3
  318.3 0.7 pad_maximum_fusion.refs_4_
  319.0 83.9 %shard_map.206 = (f32[24,2304]{1,0:T(8,128)}, f32[24,768]{1,0:T(8,128)}, f32[24,3072]{1,0:T(8,128)}, f32[96,768]{1,0:T(8,128)}, f32[8,128]{1,0:T(8,128)}) custom-call(bf16[2,2,2,2,2,24,2304]{6,5,4,3,2,1,0:T(8,128)(2,1)} %bitcast.63, bf16[2,2,2,2,2,24,768]{6,5,4,3,2,1,0:T(8,128)(2,1)} %bitcast.64, bf16[2,2,2,2,2,24,3072]{6,5,4,3,2,1,0:T(8,128)(2,1)} %bitcast.58, ...), custom_call_target="tpu_custom_call" | custom-call | bytes 28573696 | tf_op jit(solution)/shard_map/pallas_call | solution.py:228
  403.0 1.3 slice_bitcast_fusion.1
  404.3 1.3 slice_bitcast_fusion
  405.5 1.3 slice.97
  406.8 1.3 fusion.40
  408.1 1.6 copy.45
  409.7 0.7 copy.62
  410.4 0.6 copy.63
  411.0 0.7 copy.64
  411.7 0.7 copy.65
  (92 shorter events, 4.0 us)
Async XLA Ops:
  6.0 98.9 %copy-start.5 = (bf16[1024,768]{0,1:T(8,128)(2,1)}, bf16[1024,768]{0,1:T(8,128)(2,1)S(1)}, u32[]{:S(2)}) copy-start(bf16[1024,768]{0,1:T(8,128)(2,1)S(1)} %copy.32) | copy-start | bytes 4718596
  111.4 41.2 %copy-start = (bf16[1024,2304]{1,0:T(8,128)(2,1)}, bf16[1024,2304]{1,0:T(8,128)(2,1)S(1)}, u32[]{:S(2)}) copy-start(bf16[1024,2304]{1,0:T(8,128)(2,1)S(1)} %add_convert_fusion.joined_ref) | copy-start | bytes 14155780
  111.4 39.5 %copy-start.6 = (bf16[1024,768]{0,1:T(8,128)(2,1)S(1)}, bf16[1024,768]{0,1:T(8,128)(2,1)}, u32[]{:S(2)}) copy-start(bf16[1024,768]{0,1:T(8,128)(2,1)} %copy-done.5) | copy-start | bytes 4718596
  111.4 39.5 %copy-start.21 = (bf16[2,2,2,2,2,24,768]{6,5,4,3,2,1,0:T(8,128)(2,1)S(1)}, bf16[2,2,2,2,2,24,768]{6,5,4,3,2,1,0:T(8,128)(2,1)}, u32[]{:S(2)}) copy-start(bf16[2,2,2,2,2,24,768]{6,5,4,3,2,1,0:T(8,128)(2,1)} %get-tuple-element.26) | copy-start | bytes 3538948
  150.9 1.7 copy-start.3
  150.9 4.5 %slice-start = ((s8[4718592]{0:T(1024)(128)(4,1)}), s8[4194304]{0:T(1024)(128)(4,1)S(1)}, s32[]{:S(2)}) async-start(s8[4718592]{0:T(1024)(128)(4,1)} %bitcast.60), calls=%async_computation | async-start | bytes 8388608
  150.9 4.5 %slice-start.1 = ((s8[4718592]{0:T(1024)(128)(4,1)}), s8[524288]{0:T(1024)(128)(4,1)S(1)}, s32[]{:S(2)}) async-start(s8[4718592]{0:T(1024)(128)(4,1)} %bitcast.60), calls=%async_computation.1 | async-start | bytes 1048576
  152.6 11.5 %copy-start.8 = (f32[1024,768]{0,1:T(8,128)}, f32[1024,768]{0,1:T(8,128)S(1)}, u32[]{:S(2)}) copy-start(f32[1024,768]{0,1:T(8,128)S(1)} %get-tuple-element.79) | copy-start | bytes 9437188
  179.0 16.3 %copy-start.14 = (bf16[1024,768]{1,0:T(8,128)(2,1)S(1)}, bf16[1024,768]{1,0:T(8,128)(2,1)}, u32[]{:S(2)}) copy-start(bf16[1024,768]{1,0:T(8,128)(2,1)} %param.23) | copy-start | bytes 4718596
  195.3 14.6 %copy-start.22 = (bf16[1024,3072]{1,0:T(8,128)(2,1)}, bf16[1024,3072]{1,0:T(8,128)(2,1)S(1)}, u32[]{:S(2)}) copy-start(bf16[1024,3072]{1,0:T(8,128)(2,1)S(1)} %get-tuple-element.81) | copy-start | bytes 18874372
  222.7 3.9 copy-start.9
  226.7 10.1 %copy-start.12 = (f32[1024,768]{0,1:T(8,128)S(1)}, f32[1024,768]{0,1:T(8,128)}, u32[]{:S(2)}) copy-start(f32[1024,768]{0,1:T(8,128)} %copy.37) | copy-start | bytes 9437188
  242.4 2.5 copy-start.15
  244.9 3.4 copy-start.4
  248.3 43.7 %copy-start.20 = (bf16[2,2,2,2,2,24,2304]{6,5,4,3,2,1,0:T(8,128)(2,1)S(1)}, bf16[2,2,2,2,2,24,2304]{6,5,4,3,2,1,0:T(8,128)(2,1)}, u32[]{:S(2)}) copy-start(bf16[2,2,2,2,2,24,2304]{6,5,4,3,2,1,0:T(8,128)(2,1)} %get-tuple-element.24) | copy-start | bytes 10616836
  292.0 5.6 %copy-start.1 = (bf16[1024,2304]{1,0:T(8,128)(2,1)}, bf16[1024,2304]{1,0:T(8,128)(2,1)S(1)}, u32[]{:S(2)}) copy-start(bf16[1024,2304]{1,0:T(8,128)(2,1)S(1)} %shard_map.205) | copy-start | bytes 14155780
  292.0 8.9 %copy-start.7 = (bf16[1024,768]{0,1:T(8,128)(2,1)S(1)}, bf16[1024,768]{0,1:T(8,128)(2,1)}, u32[]{:S(2)}) copy-start(bf16[1024,768]{0,1:T(8,128)(2,1)} %copy-done.5) | copy-start | bytes 4718596
  297.7 3.8 copy-start.2
  311.2 2.8 copy-start.10
  313.8 2.0 copy-start.11
  313.8 2.4 copy-start.13
  403.0 6.7 %copy-start.18 = (f32[24,2304]{1,0:T(8,128)S(1)}, f32[24,2304]{1,0:T(8,128)}, u32[]{:S(2)}) copy-start(f32[24,2304]{1,0:T(8,128)} %get-tuple-element.99) | copy-start | bytes 663556
  403.0 7.4 %copy-start.19 = (f32[24,768]{1,0:T(8,128)S(1)}, f32[24,768]{1,0:T(8,128)}, u32[]{:S(2)}) copy-start(f32[24,768]{1,0:T(8,128)} %get-tuple-element.100) | copy-start | bytes 221188
  403.0 8.0 %copy-start.17 = (f32[24,3072]{1,0:T(8,128)S(1)}, f32[24,3072]{1,0:T(8,128)}, u32[]{:S(2)}) copy-start(f32[24,3072]{1,0:T(8,128)} %get-tuple-element.101) | copy-start | bytes 884740
  403.0 8.7 %copy-start.16 = (f32[96,768]{1,0:T(8,128)S(1)}, f32[96,768]{1,0:T(8,128)}, u32[]{:S(2)}) copy-start(f32[96,768]{1,0:T(8,128)} %get-tuple-element.102) | copy-start | bytes 884740
